TPU v7x, 256 devices: a whole 4x4x8 slice. The times are simulated.
256 devices in a mesh: tok: 16 (over z, core), exp: 16 (over y, x).
Axes of the slice: x: 4, y: 4, z: 8, core: 2. Of those that a mesh axis runs over, the one named last changes fastest.
Arguments:
- tokens: bfloat16 [131072, 2048], P(('tok', 'exp')), may hold values from -40 to 40
- first_factor: bfloat16 [128, 2048, 256], P('exp'), may hold values from -0.125 to 0.125
- expert_ids: int32 [131072, 8], P(('tok', 'exp')), may hold values from 0 to 127, all different within a row; in each aligned block of 512 rows (0 to 511, 512 to 1023, ...) at most 40 rows name the same one
Outputs:
- codes: bfloat16 [131072, 8, 256], P(('tok', 'exp'))
- upper_factor: float32 [128, 256, 256], P('exp')
Inputs may be any that keep to these rules, and one draw needn't show every extreme that they name: `expert_ids`: within the rows of one device (aligned blocks of 512 tokens) no expert is named more than 40 times, a bound that some block reaches; each token names 8 different experts, and every expert is named by some token.
All inputs are finite; a program needn't handle non-finite values.
Results may differ from a plain program's by a relative error of at most 0.0058.
Values may be sent and summed in bfloat16 or wider, within the bound.
No kernel may reach another device: no remote copies, remote signals or barrier semaphores. Data moves between devices by JAX's collectives and lax.ppermute only.
A program may use at most 256 MiB of HBM per device.

v0:
```python
import jax
import jax.numpy as jnp
from jax import lax
from jax.sharding import PartitionSpec as P

RIDGE = 0.1


def slot_table(id_block, experts, capacity):
    tok_rows, top_k = id_block.shape
    pair_expert = id_block.reshape(-1)
    onehots = (pair_expert[:, None] == jnp.arange(experts, dtype=jnp.int32)[None, :]).astype(
        jnp.int32
    )
    before = jnp.sum((jnp.cumsum(onehots, axis=0) - onehots) * onehots, axis=1)
    slot_index = pair_expert * capacity + before
    pair_token = jnp.arange(pair_expert.shape[0], dtype=jnp.int32) // top_k
    source = jnp.full((experts * capacity,), tok_rows, jnp.int32).at[slot_index].set(pair_token)
    return (slot_index, source)


def local(tokens, first_factor, expert_ids):
    groups = lax.axis_size("exp")
    tok_ranks = lax.axis_size("tok")
    per_group, model_dim, rank_k = first_factor.shape
    tok_rows, top_k = expert_ids.shape
    experts = groups * per_group
    capacity = tok_rows * top_k * 5 // (4 * experts)
    gram_scale = experts / (top_k * tok_rows * tok_ranks * groups)
    slot_index, source = slot_table(expert_ids, experts, capacity)
    padded = jnp.concatenate([tokens, jnp.zeros((1, model_dim), tokens.dtype)], axis=0)
    outgoing = padded[source].reshape(groups, per_group, capacity, model_dim)
    incoming = lax.all_to_all(outgoing, "exp", split_axis=0, concat_axis=0, tiled=True)
    projected = jnp.einsum(
        "slmd,ldk->slmk", incoming, first_factor, preferred_element_type=jnp.float32
    ).astype(jnp.bfloat16)
    partial_gram = gram_scale * jnp.einsum(
        "slmk,slmj->lkj", projected, projected, preferred_element_type=jnp.float32
    )
    identity = jnp.eye(rank_k, dtype=jnp.float32)
    total_gram = lax.psum(partial_gram, "tok")
    lower_factor = jnp.linalg.cholesky(total_gram + RIDGE * identity)
    rhs_columns = (
        jnp.transpose(projected, (1, 3, 0, 2))
        .reshape(per_group, rank_k, groups * capacity)
        .astype(jnp.float32)
    )
    solved = jax.vmap(
        lambda factor_one, rhs_block: jax.scipy.linalg.solve_triangular(
            factor_one, rhs_block, lower=True
        )
    )(lower_factor, rhs_columns)
    codes_here = jnp.transpose(
        solved.reshape(per_group, rank_k, groups, capacity), (2, 0, 3, 1)
    ).astype(jnp.bfloat16)
    returned = lax.all_to_all(codes_here, "exp", split_axis=0, concat_axis=0, tiled=True)
    gathered = returned.reshape(experts * capacity, rank_k)[slot_index]
    return (gathered.reshape(tok_rows, top_k, rank_k), jnp.swapaxes(lower_factor, 1, 2))


def solution(mesh):
    in_specs = (P(("tok", "exp"), None), P("exp", None, None), P(("tok", "exp"), None))
    out_specs = (P(("tok", "exp"), None, None), P("exp", None, None))
    return jax.shard_map(local, mesh=mesh, in_specs=in_specs, out_specs=out_specs, check_vma=False)
```

profile of v0, /device:TPU:1, one launch (start us, length us, event | category | flops | bytes accessed | tf_op | source)
XLA Modules:
  0.0 962.5 jit_solution(15166830196996044114)
XLA Ops:
  11.6 1.4 fusion.9
  13.1 15.5 %scatter_custom_fusion = s32[5120]{0:T(1024)S(1)} fusion(s32[4096]{0:T(1024)S(1)} %bitcast.81, s32[4096]{0:T(1024)S(1)} %add_select_fusion, s32[]{:T(128)} %constant.111.clone.1), kind=kCustom, calls=%fused_computation.61 | custom fusion | bytes 20484 | tf_op jit(solution)/shard_map/scatter | solution.py:18
  28.7 1.7 concatenate.7
  30.4 26.0 %gather_fusion = bf16[5120,2048]{1,0:T(8,128)(2,1)} fusion(bf16[513,2048]{1,0:T(8,128)(2,1)S(1)} %concatenate.7, s32[5120]{0:T(1024)S(1)} %fusion.34), kind=kCustom, calls=%fused_computation | custom fusion | bytes 41963520 | tf_op jit(solution)/shard_map/gather | solution.py:32
  56.4 238.3 %all_to_all.10 = bf16[16,8,40,2048]{3,2,1,0:T(8,128)(2,1)} all-to-all(bf16[16,8,40,2048]{3,2,1,0:T(8,128)(2,1)} %bitcast.75), channel_id=1, replica_groups=mesh['tok'=16,'exp'=16] {'exp'}, dimensions={0} | all-to-all | bytes 41943040 | tf_op jit(solution)/shard_map/all_to_all | solution.py:33
  294.7 12.3 %fusion.13 = bf16[8,16,40,256]{3,2,1,0:T(8,128)(2,1)S(1)} fusion(bf16[8,2048,256]{2,1,0:T(8,128)(2,1)} %param.4, bf16[16,8,40,2048]{3,2,1,0:T(8,128)(2,1)} %all_to_all.10), kind=kOutput, calls=%fused_computation.25 | convolution fusion | flops 5370019840 | bytes 31981568 | tf_op jit(solution)/shard_map/slmd,ldk->slmk/dot_general | solution.py:34
  307.0 2.4 bitcast_multiply_fusion
  309.6 1.5 triangular_solve.85
  311.9 111.8 %all-reduce.4.cloned.1.call-done = f32[8,256,256]{1,2,0:T(8,128)} async-done(((f32[8,256,256]{1,2,0:T(8,128)}), f32[8,256,256]{1,2,0:T(8,128)}) %all-reduce.4.cloned.1.call-update) | async-done | bytes 2097168 | tf_op jit(solution)/shard_map/psum | solution.py:41
  423.7 3.1 broadcast_add_fusion
  426.7 3.0 copy.59
  429.8 1.9 fusion.10
  431.7 1.3 copy-done.2
  433.0 94.5 %custom-call.17 = f32[8,128,128]{2,1,0:T(8,128)} custom-call(f32[8,128,128]{2,1,0:T(8,128)S(1)} %cholesky.122), custom_call_target="Cholesky" | custom-call | tf_op jit(solution)/shard_map/jit(cholesky)/cholesky | solution.py:42
  529.6 80.0 %custom-call.18 = f32[8,1,128,128]{2,3,1,0:T(8,128)} custom-call(f32[8,1,128,128]{3,2,1,0:T(8,128)} %select_bitcast_fusion), custom_call_target="InvertDiagBlocksLowerTriangular" | custom-call | tf_op jit(solution)/shard_map/jit(cholesky)/cholesky | solution.py:42
  609.7 1.8 constant_dynamic-update-slice_fusion.1
  611.5 3.1 convolution_subtract_fusion
  614.6 95.2 %custom-call.19 = f32[8,128,128]{2,1,0:T(8,128)} custom-call(f32[8,128,128]{2,1,0:T(8,128)} %convolution_subtract_fusion), custom_call_target="Cholesky" | custom-call | tf_op jit(solution)/shard_map/jit(cholesky)/cholesky | solution.py:42
  712.5 3.4 fusion.18
  716.0 5.7 while.1
  716.6 2.3 bitcast_dynamic-update-slice_fusion.2
  719.4 2.3 bitcast_dynamic-update-slice_fusion.2
  721.7 158.6 %custom-call.20 = f32[8,2,128,128]{2,3,1,0:T(8,128)} custom-call(f32[8,2,128,128]{3,2,1,0:T(8,128)} %bitcast.83), custom_call_target="InvertDiagBlocksLowerTriangular" | custom-call | tf_op jit(solution)/shard_map/vmap(jit(_solve_triangular))/triangular_solve | solution.py:49
  880.4 3.0 fusion.41
  883.3 2.5 fusion.28
  885.8 2.5 fusion.22
  888.6 2.6 copy.67
  891.2 3.5 copy.68
  894.7 6.5 all-to-all-start.1
  901.3 2.9 copy.69
  904.1 34.4 %all-to-all-done.1 = bf16[16,8,40,256]{3,2,1,0:T(8,128)(2,1)S(1)} async-done(((bf16[16,8,40,256]{3,2,1,0:T(8,128)(2,1)}), bf16[16,8,40,256]{3,2,1,0:T(8,128)(2,1)S(1)}, u32[]{:S(2)}, u32[]{:S(2)}) %all-to-all-start.1) | async-done | bytes 2621472 | tf_op jit(solution)/shard_map/all_to_all | solution.py:56
  938.6 17.0 %gather_fusion.1 = bf16[4096,256]{1,0:T(8,128)(2,1)} fusion(bf16[5120,256]{1,0:T(8,128)(2,1)S(1)} %bitcast.74, s32[4096]{0:T(1024)S(1)} %broadcast_clamp_fusion), kind=kCustom, calls=%fused_computation.1 | custom fusion | bytes 4210688 | tf_op jit(solution)/shard_map/gather | solution.py:57
  (51 shorter events, 11.6 us)
Async XLA Ops:
  7.2 416.5 %all-reduce.4.cloned.1.call-start = ((), (), s32[]{:S(2)}) async-start(), calls=%async_computation.2 | async-start | bytes 4194304 | tf_op jit(solution)/shard_map/psum | solution.py:41
  307.0 2.4 copy-start.4
  309.6 114.1 %copy-start.5 = (f32[256,256]{0,1:T(8,128)}, f32[256,256]{0,1:T(8,128)S(1)}, u32[]{:S(2)}) copy-start(f32[256,256]{0,1:T(8,128)S(1)} %fusion.33) | copy-start | bytes 786436
  426.7 3.0 copy-start
  431.7 1.3 copy-start.2
  527.5 1.3 copy-start.3
  711.2 1.3 copy-start.1
  883.3 2.5 copy-start.6
  894.7 43.9 %all-to-all-start.1 = ((bf16[16,8,40,256]{3,2,1,0:T(8,128)(2,1)}), bf16[16,8,40,256]{3,2,1,0:T(8,128)(2,1)S(1)}, u32[]{:S(2)}, u32[]{:S(2)}) async-start(bf16[16,8,40,256]{3,2,1,0:T(8,128)(2,1)} %copy.68), calls=%async_computation.1 | async-start | bytes 5242880 | tf_op jit(solution)/shard_map/all_to_all | solution.py:56
Sparse Core Ops, SparseCore 0:
  309.6 114.0 all-reduce.3
where the time goes:
time: 966 us; the launch traced here: 962 us
  other arithmetic  442 us (46%)
  blocking collectives  238 us (25%)
  waiting for transfers between devices  146 us (15%)
  local copies, waits for them, and re-layouts  86.9 us (9%)
  matrix products  27.5 us (3%)
  between operations  14.3 us (1%)
    another operation x9, other arithmetic, local(): lower_factor = jnp.linalg.cholesky(total_gram + RIDGE * identity)  272 us
    all_to_all x1, blocking collectives, local(): lax.all_to_all(outgoing, 'exp', split_axis=0, concat_axis=0, tiled=True)  238 us
    another operation x4, other arithmetic, local(): jax.scipy.linalg.solve_triangular(factor_one, rhs_block, lower=True)  159 us
    psum x1, waiting for transfers between devices, local(): total_gram = lax.psum(partial_gram, 'tok')  112 us
    all_to_all x1, waiting for transfers between devices, local(): lax.all_to_all(codes_here, 'exp', split_axis=0, concat_axis=0, tiled=True)  34.4 us
    gather x1, local copies, waits for them, and re-layouts, local(): outgoing = padded[source].reshape(groups, per_group, capacity, model_dim)  26 us
  transfers between devices with their start and end apart: 2, of which 2 were waited for; matrix products, arithmetic and copies ran while one was open for 1% of the time, Pallas kernels for 0%

commit v1 on v0

v1 whole, which is shorter than its diff:
```python
import functools

import jax
import jax.numpy as jnp
from jax import lax
from jax.experimental import pallas as pl
from jax.experimental.pallas import tpu as pltpu
from jax.sharding import Mesh
from jax.sharding import PartitionSpec as P

RIDGE = 0.1
BLOCK = 32
VMEM_BYTES = 48 * 2**20


def exact_dot(a, b, dims):
    return lax.dot_general(
        a, b, (dims, ((), ())), precision=lax.Precision.HIGHEST, preferred_element_type=jnp.float32
    )


def factor_kernel(gram_ref, upper_ref, high_ref, low_ref, work, *, block):
    experts, _, half, _ = gram_ref.shape
    size = 2 * half
    lanes = 128
    groups = lanes // block
    tiles = experts // groups
    rows_h = lax.broadcasted_iota(jnp.int32, (half, half), 0)
    cols_h = lax.broadcasted_iota(jnp.int32, (half, half), 1)
    ridge_h = jnp.where(rows_h == cols_h, RIDGE, 0.0).astype(jnp.float32)
    for e in range(experts):
        work[e, :half, :half] = gram_ref[e, 0] + ridge_h
        work[e, :half, half:] = gram_ref[e, 1]
        work[e, half:, half:] = gram_ref[e, 2] + ridge_h
    lane = lax.broadcasted_iota(jnp.int32, (block, lanes), 1)
    row = lax.broadcasted_iota(jnp.int32, (block, lanes), 0)
    unit = jnp.where(lane % block == row, 1.0, 0.0).astype(jnp.float32)
    base = (lane // block) * block
    for k in range(size // block):
        lo, hi = k * block, (k + 1) * block
        packed = [
            jnp.concatenate([work[t * groups + g, lo:hi, lo:hi] for g in range(groups)], axis=1)
            for t in range(tiles)
        ]
        inverse = [unit for _ in range(tiles)]
        scales = [jnp.ones((block, lanes), jnp.float32) for _ in range(tiles)]
        for j in range(block):
            for t in range(tiles):
                s, n = packed[t], inverse[t]
                column = jnp.take_along_axis(s, base + j, axis=1, mode="promise_in_bounds")
                pivot = column[j : j + 1, :]
                scales[t] = jnp.where(row == j, lax.rsqrt(pivot), scales[t])
                factor = jnp.where(row > j, column * (1.0 / pivot), 0.0)
                packed[t] = s - factor * s[j : j + 1, :]
                inverse[t] = n - factor * n[j : j + 1, :]
        packed = [jnp.where(lane % block >= row, s * c, 0.0) for s, c in zip(packed, scales)]
        inverse = [n * c for n, c in zip(inverse, scales)]
        for e in range(experts):
            t, g = e // groups, e % groups
            work[e, lo:hi, lo:hi] = jnp.eye(block, dtype=jnp.float32)
            strip = exact_dot(
                inverse[t][:, g * block : (g + 1) * block], work[e, lo:hi, :], ((1,), (0,))
            )
            if lo:
                upper_ref[e, lo:hi, :lo] = jnp.zeros((block, lo), jnp.float32)
            upper_ref[e, lo:hi, lo:hi] = packed[t][:, g * block : (g + 1) * block]
            work[e, lo:hi, :] = strip
            if hi < size:
                upper_ref[e, lo:hi, hi:] = strip[:, hi:]
                work[e, hi:, lo:hi] = jnp.zeros((size - hi, block), jnp.float32)
                work[e, hi:, :] = work[e, hi:, :] - exact_dot(strip[:, hi:], strip, ((0,), (0,)))
    rows = lax.broadcasted_iota(jnp.int32, (size, size), 0)
    cols = lax.broadcasted_iota(jnp.int32, (size, size), 1)
    for e in range(experts):
        whole = jnp.where(rows >= cols, work[e], 0.0)
        high = whole.astype(jnp.bfloat16)
        high_ref[e] = high
        low_ref[e] = (whole - high.astype(jnp.float32)).astype(jnp.bfloat16)


def factorize(gram_blocks):
    experts, _, half, _ = gram_blocks.shape
    size = 2 * half
    square = (experts, size, size)
    return pl.pallas_call(
        functools.partial(factor_kernel, block=BLOCK),
        out_shape=(
            jax.ShapeDtypeStruct(square, jnp.float32),
            jax.ShapeDtypeStruct(square, jnp.bfloat16),
            jax.ShapeDtypeStruct(square, jnp.bfloat16),
        ),
        scratch_shapes=[pltpu.VMEM(square, jnp.float32)],
        compiler_params=pltpu.CompilerParams(vmem_limit_bytes=VMEM_BYTES),
        name="factorize",
    )(gram_blocks)


def slot_ranks(ids, experts):
    rows = ids.shape[0]
    named = (ids[:, :, None] == jnp.arange(experts, dtype=jnp.int32)).any(axis=1)
    earlier = jnp.arange(rows)[:, None] > jnp.arange(rows)[None, :]
    rank = jnp.dot(
        earlier.astype(jnp.bfloat16), named.astype(jnp.bfloat16), preferred_element_type=jnp.float32
    )
    return jnp.where(named, rank, -1.0).astype(jnp.int32)


def reduce_gram(partial_gram):
    experts, parts, half, _ = partial_gram.shape
    cores, layers = lax.axis_size("c"), lax.axis_size("z")
    core = lax.axis_index("c")
    split = partial_gram.reshape(cores, -1, half)
    swap = [(i, (i + 1) % cores) for i in range(cores)]
    mine = lax.dynamic_index_in_dim(split, core, 0, keepdims=False)
    other = lax.dynamic_index_in_dim(split, 1 - core, 0, keepdims=False)
    mine = mine + lax.ppermute(other, "c", swap)
    pieces = lax.all_to_all(mine.reshape(layers, -1, half), "z", 0, 0, tiled=True)
    mine = lax.all_gather(jnp.sum(pieces, axis=0), "z", tiled=True)
    other = lax.ppermute(mine, "c", swap)
    whole = jnp.where(core == 0, jnp.stack([mine, other]), jnp.stack([other, mine]))
    return whole.reshape(experts, parts, half, half)


def local(tokens, first_factor, expert_ids):
    groups = lax.axis_size(("y", "x"))
    tok_ranks = lax.axis_size(("z", "c"))
    per_group, model_dim, rank_k = first_factor.shape
    tok_rows, top_k = expert_ids.shape
    experts = groups * per_group
    capacity = tok_rows * top_k * 5 // (4 * experts)
    gram_scale = experts / (top_k * tok_rows * tok_ranks * groups)
    half = rank_k // 2
    ranks = slot_ranks(expert_ids, experts)
    select = ranks.T[:, None, :] == jnp.arange(capacity, dtype=jnp.int32)[None, :, None]
    outgoing = jnp.einsum(
        "est,td->esd", select.astype(jnp.bfloat16), tokens, preferred_element_type=jnp.float32
    ).astype(jnp.bfloat16)
    incoming = lax.all_to_all(
        outgoing.reshape(groups, per_group, capacity, model_dim), ("y", "x"), 0, 0, tiled=True
    )
    projected = jnp.einsum(
        "slmd,ldk->slmk", incoming, first_factor, preferred_element_type=jnp.float32
    ).astype(jnp.bfloat16)
    partial_gram = gram_scale * jnp.einsum(
        "slmk,slmj->lkj", projected, projected, preferred_element_type=jnp.float32
    )
    partial_gram = jnp.stack(
        [
            partial_gram[:, :half, :half],
            partial_gram[:, :half, half:],
            partial_gram[:, half:, half:],
        ],
        axis=1,
    )
    upper, high, low = factorize(reduce_gram(partial_gram))
    codes = sum(
        jnp.einsum("slmk,ljk->slmj", projected, term, preferred_element_type=jnp.float32)
        for term in (high, low)
    ).astype(jnp.bfloat16)
    returned = lax.all_to_all(codes, ("y", "x"), 0, 0, tiled=True)
    own_rank = jnp.take_along_axis(ranks, expert_ids, axis=1)
    slot = (expert_ids * capacity + own_rank).reshape(-1)
    gathered = returned.reshape(experts * capacity, rank_k)[slot]
    return (gathered.reshape(tok_rows, top_k, rank_k), upper)


def solution(mesh):
    layers = mesh.shape["tok"] // 2
    side = 4
    fine = Mesh(
        mesh.devices.reshape(layers, 2, mesh.shape["exp"] // side, side), ("z", "c", "y", "x")
    )
    every = ("z", "c", "y", "x")
    in_specs = (P(every, None), P(("y", "x"), None, None), P(every, None))
    out_specs = (P(every, None, None), P(("y", "x"), None, None))
    return jax.shard_map(local, mesh=fine, in_specs=in_specs, out_specs=out_specs, check_vma=False)
```

time: 966 us -> 535 us (0.55)
  other arithmetic: 442 us -> 3.28 us
  blocking collectives: 238 us -> 51.1 us
  waiting for transfers between devices: 146 us -> 330 us
  Pallas kernels: 0 us -> 37.7 us
  local copies, waits for them, and re-layouts: 86.9 us -> 63.5 us
  starting transfers between devices: 6.57 us -> 21 us
  between operations: 14.3 us -> 0.86 us
    another operation x16 -> x1, other arithmetic: 432 us -> 0.1 us  [local(): jnp.stack([partial_gram[:, :half, :half], partial_gram[:, :half, half:],...]
    all_to_all x1 -> x2, waiting for transfers between devices: 34.4 us -> 326 us  [the longest x1 312 us: local(): lax.all_to_all(outgoing.reshape(groups, per_group, capacity, model_dim),...]
    all_to_all x1, blocking collectives: 238 us -> 30.3 us  [reduce_gram(): lax.all_to_all(mine.reshape(layers, -1, half), 'z', 0, 0, tiled=True)]
    psum x1 -> x0, waiting for transfers between devices: 112 us -> none  [local(): total_gram = lax.psum(partial_gram, 'tok')]
    pallas_call x0 -> x1, Pallas kernels: none -> 37.7 us  [factorize(): pl.pallas_call(functools.partial(factor_kernel, block=BLOCK), out_shape=(...]
    all_gather x0 -> x1, blocking collectives: none -> 20.7 us  [reduce_gram(): mine = lax.all_gather(jnp.sum(pieces, axis=0), 'z', tiled=True)]
    scatter x1 -> x0, local copies, waits for them, and re-layouts: 15.5 us -> none  [slot_table(): jnp.full((experts * capacity,), tok_rows, jnp.int32).at[slot_index]]
    reshape x0 -> x2, local copies, waits for them, and re-layouts: none -> 14.6 us  [the longest x1 14.5 us: local(): outgoing.reshape(groups, per_group, capacity, model_dim)]
  transfers between devices with their start and end apart: 2 -> 4, of which waited for: 2 -> 4; matrix products, arithmetic and copies ran while one was open for 1% -> 5% of each run, Pallas kernels for 0% -> 0%
where the time goes in v1:
time: 535 us; the launch traced here: 534 us
  waiting for transfers between devices  330 us (62%)
  local copies, waits for them, and re-layouts  63.5 us (12%)
  blocking collectives  51.1 us (10%)
  Pallas kernels  37.7 us (7%)
  matrix products  27.3 us (5%)
  starting transfers between devices  21 us (4%)
    all_to_all x1, waiting for transfers between devices, local(): lax.all_to_all(outgoing.reshape(groups, per_group, capacity, model_dim),...  312 us
    pallas_call x1, Pallas kernels, factorize(): pl.pallas_call(functools.partial(factor_kernel, block=BLOCK), out_shape=(...  37.7 us
    all_to_all x1, blocking collectives, reduce_gram(): lax.all_to_all(mine.reshape(layers, -1, half), 'z', 0, 0, tiled=True)  30.3 us
    gather x5, local copies, waits for them, and re-layouts, local(): own_rank = jnp.take_along_axis(ranks, expert_ids, axis=1)  26.1 us
    all_gather x1, blocking collectives, reduce_gram(): mine = lax.all_gather(jnp.sum(pieces, axis=0), 'z', tiled=True)  20.7 us
    gather x1, local copies, waits for them, and re-layouts, local(): gathered = returned.reshape(experts * capacity, rank_k)[slot]  18.2 us
    reshape x1, local copies, waits for them, and re-layouts, local(): outgoing.reshape(groups, per_group, capacity, model_dim)  14.5 us
    all_to_all x1, waiting for transfers between devices, local(): returned = lax.all_to_all(codes, ('y', 'x'), 0, 0, tiled=True)  14 us
  transfers between devices with their start and end apart: 4, of which 4 were waited for; matrix products, arithmetic and copies ran while one was open for 5% of the time, Pallas kernels for 0%

profile of v1, /device:TPU:1, one launch (start us, length us, event | category | flops | bytes accessed | tf_op | source)
XLA Modules:
  0.0 534.5 jit_solution(971272461916145197)
XLA Ops:
  0.6 1.0 copy.46
  1.6 2.9 fusion.12
  4.6 0.3 fusion.22
  4.9 0.1 copy.47
  5.0 11.6 %convert_bitcast_fusion = bf16[16,8,40,2048]{3,1,0,2:T(8,128)(2,1)S(1)} fusion(s32[128,512]{1,0:T(8,128)S(1)} %copy.47, bf16[512,2048]{1,0:T(8,128)(2,1)S(1)} %copy-done), kind=kOutput, calls=%fused_computation.4 | convolution fusion | flops 10750525440 | bytes 23330816 | tf_op jit(solution)/shard_map/est,td->esd/dot_general | solution.py:135
  16.6 14.5 %copy.48 = bf16[16,8,40,2048]{3,2,1,0:T(8,128)(2,1)} copy(bf16[16,8,40,2048]{3,1,0,2:T(8,128)(2,1)S(1)} %convert_bitcast_fusion) | data formatting | bytes 41943040 | tf_op jit(solution)/shard_map/reshape | solution.py:139
  31.1 7.6 %all-to-all-start = ((bf16[16,8,40,2048]{3,2,1,0:T(8,128)(2,1)}), bf16[16,8,40,2048]{3,2,1,0:T(8,128)(2,1)}, u32[]{:S(2)}, u32[]{:S(2)}) async-start(bf16[16,8,40,2048]{3,2,1,0:T(8,128)(2,1)} %copy.48), calls=%async_computation | async-start | bytes 41943040 | tf_op jit(solution)/shard_map/all_to_all | solution.py:138
  38.7 311.9 %all-to-all-done = bf16[16,8,40,2048]{3,2,1,0:T(8,128)(2,1)} async-done(((bf16[16,8,40,2048]{3,2,1,0:T(8,128)(2,1)}), bf16[16,8,40,2048]{3,2,1,0:T(8,128)(2,1)}, u32[]{:S(2)}, u32[]{:S(2)}) %all-to-all-start) | async-done | bytes 20971552 | tf_op jit(solution)/shard_map/all_to_all | solution.py:138
  350.6 12.3 %fusion.15 = bf16[8,16,40,256]{3,2,1,0:T(8,128)(2,1)S(1)} fusion(bf16[8,2048,256]{2,1,0:T(8,128)(2,1)} %param.4, bf16[16,8,40,2048]{3,2,1,0:T(8,128)(2,1)} %all-to-all-done), kind=kOutput, calls=%fused_computation.20 | convolution fusion | flops 5370019840 | bytes 31981568 | tf_op jit(solution)/shard_map/slmd,ldk->slmk/dot_general | solution.py:141
  362.9 1.2 bitcast_multiply_fusion
  364.1 0.3 copy-done.2
  364.4 0.2 slice_bitcast_fusion.2
  364.8 0.9 dynamic-slice_bitcast_fusion
  365.7 1.8 collective-permute-start
  367.5 2.1 collective-permute-done
  369.7 30.3 %all_to_all.15 = f32[8,192,128]{2,1,0:T(8,128)S(1)} all-to-all(f32[8,192,128]{2,1,0:T(8,128)S(1)} %bitcast.66), channel_id=1, replica_groups=mesh['z'=8,'c'=2,'y'=4,'x'=4] {'z'}, dimensions={0} | all-to-all | bytes 1572864 | tf_op jit(solution)/shard_map/all_to_all | solution.py:117
  400.1 20.7 %all_gather.3 = f32[1536,128]{1,0:T(8,128)S(1)} all-gather(f32[192,128]{1,0:T(8,128)S(1)} %reduce_sum.9), channel_id=1, replica_groups=mesh['z'=8,'c'=2,'y'=4,'x'=4] {'z'}, dimensions={0}, use_global_device_ids=true | all-gather | bytes 884736 | tf_op jit(solution)/shard_map/all_gather | solution.py:118
  420.9 6.9 %collective-permute-start.1 = (f32[1536,128]{1,0:T(8,128)S(1)}, f32[1536,128]{1,0:T(8,128)S(1)}, u32[]{:S(2)}, u32[]{:S(2)}) collective-permute-start(f32[1536,128]{1,0:T(8,128)S(1)} %all_gather.3), channel_id=1, source_target_pairs={{0,16},{16,0},{1,17},{17,1},{2,18},{18,2},{3,19},{19,3},{4,20},{20... | collective-permute-start | bytes 2359304 | tf_op jit(solution)/shard_map/ppermute | solution.py:119
  427.8 1.9 collective-permute-done.1
  429.8 37.7 %factorize.1 = (f32[8,256,256]{2,1,0:T(8,128)}, bf16[8,256,256]{2,1,0:T(8,128)(2,1)S(1)}, bf16[8,256,256]{2,1,0:T(8,128)(2,1)S(1)}) custom-call(f32[8,3,128,128]{3,2,1,0:T(8,128)S(1)} %bitcast.62), custom_call_target="tpu_custom_call" | custom-call | tf_op jit(solution)/shard_map/factorize/pallas_call | solution.py:85
  467.5 0.9 fusion.5
  468.4 1.0 fusion.4
  469.4 1.8 copy.51
  471.2 4.6 all-to-all-start.2
  475.8 0.1 copy.52
  476.0 0.2 reshape.81
  476.1 25.6 %gather_fusion.1 = s32[4096]{0:T(1024)S(1)} fusion(s32[512,128]{1,0:T(8,128)S(1)} %fusion.22, s32[4096]{0:T(1024)S(1)} %reshape.81), kind=kCustom, calls=%fused_computation.1 | custom fusion | bytes 65536 | tf_op jit(solution)/shard_map/jit(take_along_axis)/gather | solution.py:161
  501.7 0.2 reshape.84
  502.0 0.1 copy.54
  502.1 0.2 reshape.71
  502.4 14.0 %all-to-all-done.2 = bf16[16,8,40,256]{3,2,1,0:T(8,128)(2,1)} async-done(((bf16[16,8,40,256]{3,2,1,0:T(8,128)(2,1)}), bf16[16,8,40,256]{3,2,1,0:T(8,128)(2,1)}, u32[]{:S(2)}, u32[]{:S(2)}) %all-to-all-start.2) | async-done | bytes 2621472 | tf_op jit(solution)/shard_map/all_to_all | solution.py:160
  516.3 18.2 %gather_fusion = bf16[4096,256]{1,0:T(8,128)(2,1)} fusion(bf16[5120,256]{1,0:T(8,128)(2,1)} %bitcast.23, s32[4096]{0:T(1024)S(1)} %broadcast_clamp_fusion), kind=kCustom, calls=%fused_computation | custom fusion | bytes 4210688 | tf_op jit(solution)/shard_map/gather | solution.py:163
  (19 shorter events, 0.6 us)
Async XLA Ops:
  0.6 4.4 copy-start
  31.1 319.5 %all-to-all-start = ((bf16[16,8,40,2048]{3,2,1,0:T(8,128)(2,1)}), bf16[16,8,40,2048]{3,2,1,0:T(8,128)(2,1)}, u32[]{:S(2)}, u32[]{:S(2)}) async-start(bf16[16,8,40,2048]{3,2,1,0:T(8,128)(2,1)} %copy.48), calls=%async_computation | async-start | bytes 41943040 | tf_op jit(solution)/shard_map/all_to_all | solution.py:138
  362.9 1.5 copy-start.2
  365.7 3.9 collective-permute-start
  420.9 8.8 %collective-permute-start.1 = (f32[1536,128]{1,0:T(8,128)S(1)}, f32[1536,128]{1,0:T(8,128)S(1)}, u32[]{:S(2)}, u32[]{:S(2)}) collective-permute-start(f32[1536,128]{1,0:T(8,128)S(1)} %all_gather.3), channel_id=1, source_target_pairs={{0,16},{16,0},{1,17},{17,1},{2,18},{18,2},{3,19},{19,3},{4,20},{20... | collective-permute-start | bytes 2359304 | tf_op jit(solution)/shard_map/ppermute | solution.py:119
  429.7 37.8 %copy-start.3 = (bf16[8,16,40,256]{3,2,1,0:T(8,128)(2,1)S(1)}, bf16[8,16,40,256]{3,2,1,0:T(8,128)(2,1)}, u32[]{:S(2)}) copy-start(bf16[8,16,40,256]{3,2,1,0:T(8,128)(2,1)} %copy-done.2) | copy-start | bytes 7864324
  471.2 4.6 copy-start.4
  471.2 45.1 %all-to-all-start.2 = ((bf16[16,8,40,256]{3,2,1,0:T(8,128)(2,1)}), bf16[16,8,40,256]{3,2,1,0:T(8,128)(2,1)}, u32[]{:S(2)}, u32[]{:S(2)}) async-start(bf16[16,8,40,256]{3,2,1,0:T(8,128)(2,1)} %copy.51), calls=%async_computation.2 | async-start | bytes 5242880 | tf_op jit(solution)/shard_map/all_to_all | solution.py:160
  516.3 18.2 %copy-start.1 = (bf16[512,2048]{1,0:T(8,128)(2,1)S(1)}, bf16[512,2048]{1,0:T(8,128)(2,1)}, u32[]{:S(2)}) copy-start(bf16[512,2048]{1,0:T(8,128)(2,1)} %param.3) | copy-start | bytes 6291460
